TPU v7x, 32 devices: a whole 2x2x4 slice. The times are simulated.
32 devices in a mesh: side: 2 (over y), row: 4 (over z), col: 4 (over x, core).
Axes of the slice: x: 2, y: 2, z: 4, core: 2. Of those that a mesh axis runs over, the one named last changes fastest.
Arguments:
- queries: bfloat16 [64, 8192], P(('row', 'col')), may hold values from -4.5 to 16
- new_entries: bfloat16 [64, 2048], P(('row', 'col')), may hold values from -4.5 to 15.875
- cache_keys: bfloat16 [2, 64, 256, 1024], P('side', ('row', 'col')), may hold values from -4.5 to 16
- cache_values: bfloat16 [2, 64, 256, 1024], P('side', ('row', 'col')), may hold values from -6 to 6
- lengths: int32 [64], P(('row', 'col')), may hold values from 1 to 256, 4096 in all
- residual: bfloat16 [64, 8192], P(None, 'col'), may hold values from -16 to 16
- norm_gain: bfloat16 [8192], P('col'), may hold values from 0.099609375 to 1.8984375
- out_weight: bfloat16 [2, 8192, 8192], P('side', 'row', 'col'), may hold values from -0.125 to 0.125
- gate_weight: bfloat16 [2, 8192, 14336], P('side', 'col', 'row'), may hold values from -0.0625 to 0.0625
- up_weight: bfloat16 [2, 8192, 14336], P('side', 'col', 'row'), may hold values from -0.0625 to 0.0625
- down_weight: bfloat16 [2, 14336, 8192], P('side', 'row', 'col'), may hold values from -0.046875 to 0.046875
Outputs:
- layer_out: bfloat16 [64, 8192], P(('row', 'col'), 'side')
All inputs are finite; a program needn't handle non-finite values. No bound on the sum of `lengths` on one device may be relied on, other than what follows from the above.
Results may differ from a plain program's by a relative error of at most 0.025.
Values may be sent and summed in bfloat16 or wider, within the bound.
A program may use at most 128 MiB of HBM per device.

v0:
```python
import jax
import jax.numpy as jnp
from jax import lax
from jax.sharding import PartitionSpec as P

D = 8192
H = 64
KVH = 8
HD = 128
ORIG = 64


rope_theta = 500000.0
stretch_factor = 8.0
eps = 1e-05


def from_behind(value, axis, steps):
    count = lax.axis_size(axis)
    first, last = (max(0, -steps), min(count, count - steps))
    return lax.ppermute(value, axis, [(source, source + steps) for source in range(first, last)])


def frequencies(lengths):
    seq = lengths.astype(jnp.float32) + 1.0
    stretch = jnp.maximum(stretch_factor * seq / ORIG - (stretch_factor - 1.0), 1.0)
    log_base = jnp.log(jnp.float32(rope_theta)) + HD / (HD - 2.0) * jnp.log(stretch)
    expo = jnp.arange(HD // 2).astype(jnp.float32) * (2.0 / HD)
    return jnp.exp(-expo[None, :] * log_base[:, None])


def rotary(vec, angles):
    half = vec.shape[-1] // 2
    first = vec[..., :half]
    second = vec[..., half:]
    cosine = jnp.cos(angles)
    sine = jnp.sin(angles)
    return jnp.concatenate(
        [first * cosine - second * sine, second * cosine + first * sine], axis=-1
    )


def attention(queries, new_entries, keys, values, lengths):
    slots = queries.shape[0]
    span = keys.shape[1]
    per_group = H // KVH
    freqs = frequencies(lengths)
    angle_new = lengths.astype(jnp.float32)[:, None] * freqs
    angle_cache = jnp.arange(span).astype(jnp.float32)[None, :, None] * freqs[:, None, :]
    query_rot = rotary(
        queries.astype(jnp.float32).reshape(slots, H, HD), angle_new[:, None, :]
    ).astype(jnp.bfloat16)
    query_rot = query_rot.reshape(slots, KVH, per_group, HD)
    key_fresh = new_entries[:, : KVH * HD].astype(jnp.float32).reshape(slots, KVH, HD)
    value_fresh = new_entries[:, KVH * HD :].astype(jnp.float32).reshape(slots, KVH, HD)
    key_new_rot = rotary(key_fresh, angle_new[:, None, :]).astype(jnp.bfloat16)
    key_rot = rotary(
        keys.astype(jnp.float32).reshape(slots, span, KVH, HD), angle_cache[:, :, None, :]
    ).astype(jnp.bfloat16)
    scale = HD ** (-0.5)
    scores = (
        jnp.einsum("sgqd,scgd->sgqc", query_rot, key_rot, preferred_element_type=jnp.float32)
        * scale
    )
    own_score = (
        jnp.einsum("sgqd,sgd->sgq", query_rot, key_new_rot, preferred_element_type=jnp.float32)
        * scale
    )
    valid_mask = (jnp.arange(span)[None, :] < lengths[:, None])[:, None, None, :]
    highest = jnp.maximum(jnp.max(jnp.where(valid_mask, scores, -1e30), axis=-1), own_score)
    weights = jnp.where(valid_mask, jnp.exp(scores - highest[..., None]), 0.0)
    own_weight = jnp.exp(own_score - highest)
    totals = jnp.sum(weights, axis=-1) + own_weight
    weights16 = weights.astype(jnp.bfloat16)
    mixed = jnp.einsum(
        "sgqc,scgd->sgqd",
        weights16,
        values.reshape(slots, span, KVH, HD),
        preferred_element_type=jnp.float32,
    )
    mixed = mixed + own_weight[..., None] * value_fresh[:, :, None, :]
    return (mixed / totals[..., None]).reshape(slots, H * HD).astype(jnp.bfloat16)


def local(
    queries,
    new_entries,
    cache_keys,
    cache_values,
    lengths,
    residual,
    norm_gain,
    out_weight,
    gate_weight,
    up_weight,
    down_weight,
):
    attended = attention(queries, new_entries, cache_keys[0], cache_values[0], lengths)
    slot_count = attended.shape[0]
    row_count = lax.axis_size("row")
    col_count = lax.axis_size("col")
    head_block = attended.shape[1] // row_count
    split_heads = attended.reshape(slot_count, row_count, head_block)
    moved = from_behind(split_heads, "side", 1)
    blocks = lax.all_to_all(moved, "row", split_axis=1, concat_axis=0, tiled=True)
    sectioned = blocks.reshape(row_count, 1, slot_count, head_block)
    out_block = out_weight[0]
    partial_value = jnp.einsum(
        "akjd,de->akje",
        lax.all_gather(sectioned, "col", axis=1, tiled=True),
        out_block,
        preferred_element_type=jnp.float32,
    )
    col_width = out_block.shape[1]
    total_rows = row_count * col_count * slot_count
    projected = lax.psum(
        partial_value.reshape(total_rows, col_width).astype(jnp.bfloat16), "row"
    ).astype(jnp.float32)
    stream = residual.astype(jnp.float32) + projected
    squares = lax.psum(jnp.sum(stream * stream, axis=1), "col")
    inv_rms = lax.rsqrt(squares / D + eps)
    normed = (stream * inv_rms[:, None] * norm_gain.astype(jnp.float32)[None, :]).astype(
        jnp.bfloat16
    )
    gate_block = gate_weight[0]
    up_block = up_weight[0]
    down_block = down_weight[0]
    gate_part = jnp.dot(normed, gate_block, preferred_element_type=jnp.float32)
    up_part = jnp.dot(normed, up_block, preferred_element_type=jnp.float32)
    gate_total, up_total = (
        lax.psum(gate_part.astype(jnp.bfloat16), "col").astype(jnp.float32),
        lax.psum(up_part.astype(jnp.bfloat16), "col").astype(jnp.float32),
    )
    hidden = (jax.nn.silu(gate_total) * up_total).astype(jnp.bfloat16)
    down_part = jnp.dot(hidden, down_block, preferred_element_type=jnp.float32)
    down_total = lax.psum(down_part.astype(jnp.bfloat16), "row").astype(jnp.float32)
    final = (stream + down_total).astype(jnp.bfloat16)
    group_rows = col_count * slot_count
    mine_rows = lax.dynamic_slice_in_dim(final, lax.axis_index("row") * group_rows, group_rows, 0)
    slot_rows = lax.all_to_all(mine_rows, "col", split_axis=0, concat_axis=1, tiled=True)
    half_width = slot_rows.shape[1] // 2
    returned = from_behind(slot_rows[:, :half_width], "side", -1)
    return jnp.where(lax.axis_index("side") == 0, returned, slot_rows[:, half_width:])


def solution(mesh):
    in_specs = (
        P(("row", "col"), None),
        P(("row", "col"), None),
        P("side", ("row", "col"), None, None),
        P("side", ("row", "col"), None, None),
        P(("row", "col")),
        P(None, "col"),
        P("col"),
        P("side", "row", "col"),
        P("side", "col", "row"),
        P("side", "col", "row"),
        P("side", "row", "col"),
    )
    out_specs = P(("row", "col"), "side")
    return jax.shard_map(local, mesh=mesh, in_specs=in_specs, out_specs=out_specs, check_vma=False)
```

profile of v0, /device:TPU:0, one launch (start us, length us, event | category | flops | bytes accessed | tf_op | source)
XLA Modules:
  0.0 219.9 jit_solution(17289604653617390214)
XLA Ops:
  6.5 0.7 convert_element_type.82
  7.2 0.7 multiply_add_fusion
  7.9 0.7 iota_compare_fusion
  8.6 2.8 %copy.23 = bf16[1,4,256,1024]{2,3,1,0:T(8,128)(2,1)S(1)} copy(bf16[1,4,256,1024]{3,2,1,0:T(8,128)(2,1)} %param.13) | data formatting | bytes 4194304 | tf_op args[2]
  11.5 2.5 %fusion.61 = (f32[4,256,8,64]{1,3,2,0:T(8,128)}, f32[4,256,8,64]{1,3,2,0:T(8,128)}) fusion(bf16[4,256,8,128]{1,3,2,0:T(8,128)(2,1)S(1)} %bitcast.58), kind=kLoop, calls=%fused_computation.78 | loop fusion | bytes 8388608 | tf_op jit(solution)/shard_map/slice | solution.py:35
  14.0 3.9 %copy.32 = f32[4,256,8,64]{3,1,2,0:T(8,128)} copy(f32[4,256,8,64]{1,3,2,0:T(8,128)} %get-tuple-element.12) | data formatting | bytes 4194304
  17.9 2.7 %copy.33 = f32[4,256,8,64]{3,1,2,0:T(8,128)} copy(f32[4,256,8,64]{1,3,2,0:T(8,128)S(1)} %copy-done) | data formatting | bytes 4194304
  20.7 0.0 copy-done.4
  20.8 0.1 multiply_cosine_fusion.1
  20.9 0.1 fusion.52
  21.0 0.1 subtract_convert_fusion.2
  21.1 1.9 multiply_cosine_fusion
  23.0 0.1 maximum_bitcast_fusion
  23.0 0.2 fusion.54
  23.3 4.7 %subtract_convert_fusion = (bf16[4,256,8,64]{3,1,2,0:T(8,128)(2,1)S(1)}, bf16[4,256,8,64]{3,1,2,0:T(8,128)(2,1)S(1)}) fusion(f32[4,256,8,64]{3,1,2,0:T(8,128)} %copy.33, f32[4,256,8,64]{3,1,2,0:T(8,128)} %copy.32, f32[4,256,64]{2,1,0:T(8,128)S(1)} %get-tuple-element.22, f32[4,256,64]{2,1,0:T(8,128)S(1)} %get-tuple-element.21), kind=kLoop, calls=%fused_computation.11 | loop fusion | flops 4194304 | bytes 6815744 | tf_op jit(solution)/shard_map/convert.6
  28.0 0.0 copy-start.3
  28.0 1.3 select_reduce_fusion
  29.4 0.2 fusion.45
  29.6 0.6 copy.36
  30.2 0.4 fusion.35
  30.7 0.1 copy.27
  30.8 4.9 %collective-permute-start = (bf16[4,4,2048]{2,0,1:T(4,128)(2,1)S(1)}, bf16[4,4,2048]{2,0,1:T(4,128)(2,1)S(1)}, u32[]{:S(2)}, u32[]{:S(2)}) collective-permute-start(bf16[4,4,2048]{2,0,1:T(4,128)(2,1)S(1)} %copy.27), channel_id=1, source_target_pairs={{0,16},{1,17},{2,18},{3,19},{4,20},{5,21},{6,22},{7,23},{8,24},{9,... | collective-permute-start | bytes 196616 | tf_op jit(solution)/shard_map/ppermute | solution.py:21
  35.7 1.9 collective-permute-done
  37.6 10.4 %all_to_all.34 = bf16[4,4,2048]{2,0,1:T(4,128)(2,1)S(1)} all-to-all(bf16[4,4,2048]{2,0,1:T(4,128)(2,1)S(1)} %collective-permute-done), channel_id=1, replica_groups=mesh['side'=2,'row'=4,'col'=4] {'row'}, dimensions={1} | all-to-all | bytes 131072 | tf_op jit(solution)/shard_map/all_to_all | solution.py:105
  48.0 0.1 copy.28
  48.0 5.8 %all-gather = bf16[4,16,1,2048]{3,0,2,1:T(4,128)(2,1)S(1)} all-gather(bf16[4,4,1,2048]{3,0,2,1:T(4,128)(2,1)S(1)} %copy.28), channel_id=2, replica_groups=mesh['side'=2,'row'=4,'col'=4] {'col'}, dimensions={1}, use_global_device_ids=true | all-gather | bytes 327680 | tf_op jit(solution)/shard_map/all_gather | solution.py:110
  53.8 0.1 copy.29
  54.0 0.0 copy-start.6
  54.0 0.0 copy-start.1
  54.0 5.7 %fusion.17 = bf16[64,2048]{1,0:T(8,128)(2,1)} fusion(bf16[64,2048]{1,0:T(8,128)(2,1)S(1)} %bitcast.59, bf16[1,2048,2048]{2,1,0:T(8,128)(2,1)} %param.18), kind=kOutput, calls=%fused_computation.13 | convolution fusion | flops 537001984 | bytes 8912896 | tf_op jit(solution)/shard_map/akjd,de->akje/dot_general | solution.py:108
  59.7 0.0 all-reduce.5.cloned.1.call-update
  59.7 0.0 all-reduce.9.cloned.1.call-start
  59.8 34.9 %all-reduce.5.cloned.1.call-done = bf16[64,2048]{1,0:T(8,128)(2,1)} async-done(((bf16[64,2048]{1,0:T(8,128)(2,1)}), bf16[64,2048]{1,0:T(8,128)(2,1)}) %all-reduce.5.cloned.1.call-update) | async-done | bytes 262160 | tf_op jit(solution)/shard_map/psum | solution.py:116
  94.6 1.1 multiply_reduce_fusion
  95.8 5.8 %psum.36 = f32[64]{0:T(128)S(1)} all-reduce(f32[64]{0:T(128)S(1)} %get-tuple-element.13), channel_id=1, replica_groups=mesh['side'=2,'row'=4,'col'=4] {'col'}, use_global_device_ids=true, to_apply=%region_4.5 | all-reduce | flops 64 | bytes 512 | tf_op jit(solution)/shard_map/psum | solution.py:120
  101.6 8.8 %fusion.8 = bf16[64,3584]{1,0:T(8,128)(2,1)} fusion(bf16[1,2048,3584]{2,1,0:T(8,128)(2,1)} %param.19, f32[2048]{0:T(1024)S(1)} %convert_element_type.92, f32[64]{0:T(128)S(1)} %add_rsqrt_fusion, bf16[64,2048]{1,0:T(8,128)(2,1)} %all-reduce.5.cloned.1.call-done, bf16[64,2048]{1,0:T(8,128)(2,1)S(1)} %copy-done.1), kind=kOutput, calls=%fused_computation.8 | convolution fusion | flops 940539904 | bytes 15671552 | tf_op jit(solution)/shard_map/dot_general | solution.py:128
  110.5 8.7 %fusion.11 = bf16[64,3584]{1,0:T(8,128)(2,1)} fusion(bf16[1,2048,3584]{2,1,0:T(8,128)(2,1)} %param.20, f32[2048]{0:T(1024)S(1)} %convert_element_type.92, f32[64]{0:T(128)S(1)} %add_rsqrt_fusion, bf16[64,2048]{1,0:T(8,128)(2,1)S(1)} %copy-done.2, bf16[64,2048]{1,0:T(8,128)(2,1)S(1)} %copy-done.1), kind=kOutput, calls=%fused_computation.9 | convolution fusion | flops 940539904 | bytes 15671552 | tf_op jit(solution)/shard_map/dot_general | solution.py:129
  119.2 0.0 all-reduce.9.cloned.1.call-update
  119.2 0.0 all-reduce.7.cloned.1.call-start
  119.3 35.5 %all-reduce.9.cloned.1.call-done = (bf16[64,3584]{1,0:T(8,128)(2,1)}, bf16[64,3584]{1,0:T(8,128)(2,1)}) async-done(((bf16[64,3584]{1,0:T(8,128)(2,1)}, bf16[64,3584]{1,0:T(8,128)(2,1)}), (bf16[64,3584]{1,0:T(8,128)(2,1)}, bf16[64,3584]{1,0:T(8,128)(2,1)})) %all-reduce.9.cloned.1.call-update) | async-done | bytes 917520 | tf_op jit(solution)/shard_map/psum | solution.py:132
  154.7 8.8 %fusion.14 = bf16[64,2048]{1,0:T(8,128)(2,1)} fusion(bf16[1,3584,2048]{2,1,0:T(8,128)(2,1)} %param.21, bf16[64,3584]{1,0:T(8,128)(2,1)} %get-tuple-element.5, bf16[64,3584]{1,0:T(8,128)(2,1)} %get-tuple-element.6), kind=kOutput, calls=%fused_computation.12 | convolution fusion | flops 941490176 | bytes 15859712 | tf_op jit(solution)/shard_map/dot_general | solution.py:135
  163.6 0.0 all-reduce.7.cloned.1.call-update
  163.6 35.7 %all-reduce.7.cloned.1.call-done = bf16[64,2048]{1,0:T(8,128)(2,1)} async-done(((bf16[64,2048]{1,0:T(8,128)(2,1)}), bf16[64,2048]{1,0:T(8,128)(2,1)}) %all-reduce.7.cloned.1.call-update) | async-done | bytes 262160 | tf_op jit(solution)/shard_map/psum | solution.py:136
  199.4 0.9 fusion.48
  200.2 6.7 %all_to_all.35 = bf16[4,4,2048]{2,1,0:T(4,128)(2,1)S(1)} all-to-all(bf16[4,4,2048]{2,1,0:T(4,128)(2,1)S(1)} %all_to_all.28), channel_id=1, replica_groups=mesh['side'=2,'row'=4,'col'=4] {'col'}, dimensions={0} | all-to-all | bytes 131072 | tf_op jit(solution)/shard_map/all_to_all | solution.py:140
  206.9 1.3 collective-permute-start.1
  208.2 4.5 %collective-permute-done.1 = bf16[4,4096]{1,0:T(4,128)(2,1)S(1)} collective-permute-done((bf16[4,4096]{1,0:T(4,128)(2,1)S(1)}, bf16[4,4096]{1,0:T(4,128)(2,1)S(1)}, u32[]{:S(2)}, u32[]{:S(2)}) %collective-permute-start.1) | collective-permute-done | bytes 32800 | tf_op jit(solution)/shard_map/ppermute | solution.py:21
  212.7 0.6 slice_select_fusion
  (24 shorter events, 0.2 us)
Async XLA Ops:
  6.5 88.1 %all-reduce.5.cloned.1.call-start = ((), (), s32[]{:S(2)}) async-start(), calls=%async_computation.2 | async-start | bytes 524288 | tf_op jit(solution)/shard_map/psum | solution.py:116
  14.0 3.9 %copy-start = (f32[4,256,8,64]{1,3,2,0:T(8,128)S(1)}, f32[4,256,8,64]{1,3,2,0:T(8,128)}, u32[]{:S(2)}) copy-start(f32[4,256,8,64]{1,3,2,0:T(8,128)} %get-tuple-element.11) | copy-start | bytes 6291460
  17.9 2.8 %copy-start.4 = (bf16[4,8192]{1,0:T(4,128)(2,1)S(1)}, bf16[4,8192]{1,0:T(4,128)(2,1)}, u32[]{:S(2)}) copy-start(bf16[4,8192]{1,0:T(4,128)(2,1)} %param.11) | copy-start | bytes 196612
  17.9 2.8 %copy-start.5 = (bf16[4,2048]{1,0:T(4,128)(2,1)S(1)}, bf16[4,2048]{1,0:T(4,128)(2,1)}, u32[]{:S(2)}) copy-start(bf16[4,2048]{1,0:T(4,128)(2,1)} %param.12) | copy-start | bytes 49156
  28.0 1.6 copy-start.3
  30.8 6.8 %collective-permute-start = (bf16[4,4,2048]{2,0,1:T(4,128)(2,1)S(1)}, bf16[4,4,2048]{2,0,1:T(4,128)(2,1)S(1)}, u32[]{:S(2)}, u32[]{:S(2)}) collective-permute-start(bf16[4,4,2048]{2,0,1:T(4,128)(2,1)S(1)} %copy.27), channel_id=1, source_target_pairs={{0,16},{1,17},{2,18},{3,19},{4,20},{5,21},{6,22},{7,23},{8,24},{9,... | collective-permute-start | bytes 196616 | tf_op jit(solution)/shard_map/ppermute | solution.py:21
  54.0 5.8 %copy-start.6 = (bf16[2048]{0:T(1024)(128)(2,1)S(1)}, bf16[2048]{0:T(1024)(128)(2,1)}, u32[]{:S(2)}) copy-start(bf16[2048]{0:T(1024)(128)(2,1)} %param.17) | copy-start | bytes 12292
  54.0 40.7 %copy-start.1 = (bf16[64,2048]{1,0:T(8,128)(2,1)S(1)}, bf16[64,2048]{1,0:T(8,128)(2,1)}, u32[]{:S(2)}) copy-start(bf16[64,2048]{1,0:T(8,128)(2,1)} %param.16) | copy-start | bytes 786436
  59.7 95.0 %all-reduce.9.cloned.1.call-start = ((), (), s32[]{:S(2)}) async-start(), calls=%async_computation.4 | async-start | bytes 1835008 | tf_op jit(solution)/shard_map/psum | solution.py:132
  101.6 8.8 %copy-start.2 = (bf16[64,2048]{1,0:T(8,128)(2,1)S(1)}, bf16[64,2048]{1,0:T(8,128)(2,1)}, u32[]{:S(2)}) copy-start(bf16[64,2048]{1,0:T(8,128)(2,1)} %all-reduce.5.cloned.1.call-done) | copy-start | bytes 786436
  119.2 80.1 %all-reduce.7.cloned.1.call-start = ((), (), s32[]{:S(2)}) async-start(), calls=%async_computation.3 | async-start | bytes 524288 | tf_op jit(solution)/shard_map/psum | solution.py:136
  206.9 5.8 %collective-permute-start.1 = (bf16[4,4096]{1,0:T(4,128)(2,1)S(1)}, bf16[4,4096]{1,0:T(4,128)(2,1)S(1)}, u32[]{:S(2)}, u32[]{:S(2)}) collective-permute-start(bf16[4,4096]{1,0:T(4,128)(2,1)S(1)} %slice.46), channel_id=1, source_target_pairs={{16,0},{17,1},{18,2},{19,3},{20,4},{21,5},{22,6},{23,7},{24,8},{25... | collective-permute-start | bytes 98312 | tf_op jit(solution)/shard_map/ppermute | solution.py:21
Sparse Core Ops, SparseCore 0:
  59.8 34.7 all-reduce.4
  119.3 35.3 all-reduce.8
  163.7 35.5 all-reduce.6
where the time goes:
time: 220 us
  waiting for transfers between devices  112 us (51%)
  matrix products  34.1 us (16%)
  blocking collectives  28.7 us (13%)
  between operations  13.3 us (6%)
  local copies, waits for them, and re-layouts  13.1 us (6%)
  other arithmetic  11.9 us (5%)
  starting transfers between devices  6.25 us (3%)
    psum x1, waiting for transfers between devices, local(): lax.psum(down_part.astype(jnp.bfloat16), 'row').astype(jnp.float32)  35.7 us
    psum x1, waiting for transfers between devices, local(): lax.psum(up_part.astype(jnp.bfloat16), 'col').astype(jnp.float32)  35.5 us
    psum x1, waiting for transfers between devices, local(): lax.psum(partial_value.reshape(total_rows, col_width).astype(jnp.bfloat16...  34.9 us
    all_to_all x1, blocking collectives, local(): lax.all_to_all(moved, 'row', split_axis=1, concat_axis=0, tiled=True)  10.4 us
    unnamed x19, local copies, waits for them, and re-layouts  10.2 us
    dot_general x1, matrix products, local(): down_part = jnp.dot(hidden, down_block, preferred_element_type=jnp.float32)  8.84 us
    dot_general x1, matrix products, local(): gate_part = jnp.dot(normed, gate_block, preferred_element_type=jnp.float32)  8.84 us
    dot_general x1, matrix products, local(): up_part = jnp.dot(normed, up_block, preferred_element_type=jnp.float32)  8.72 us
  transfers between devices with their start and end apart: 5, of which 5 were waited for; matrix products, arithmetic and copies ran while one was open for 0% of the time, Pallas kernels for 0%

commit v1 on v0

--- a/solution.py
+++ b/solution.py
@@ -1,6 +1,8 @@
 import jax
 import jax.numpy as jnp
 from jax import lax
+from jax.experimental import pallas as pl
+from jax.experimental.pallas import tpu as pltpu
 from jax.sharding import PartitionSpec as P
 
 D = 8192
@@ -13,12 +15,6 @@
 rope_theta = 500000.0
 stretch_factor = 8.0
 eps = 1e-05
-
-
-def from_behind(value, axis, steps):
-    count = lax.axis_size(axis)
-    first, last = (max(0, -steps), min(count, count - steps))
-    return lax.ppermute(value, axis, [(source, source + steps) for source in range(first, last)])
 
 
 def frequencies(lengths):
@@ -82,6 +78,422 @@
     return (mixed / totals[..., None]).reshape(slots, H * HD).astype(jnp.bfloat16)
 
 
+MESH = pl.DeviceIdType.MESH
+F32 = jnp.float32
+BF16 = jnp.bfloat16
+
+
+def tile_of(width):
+    return next(t for t in (512, 256, 128) if width % t == 0)
+
+
+def layer_kernel(
+    rows, cols, att, residual, gain, out_hbm, gate_hbm, up_hbm, down_hbm, out,
+    w_out, w_gate, w_up, w_down,
+    xg, xf, xb, part, rs_in, stream, sq_out, sq_in, inv_all, xs,
+    gu, core_in, sum_out, x_in, hid, acc, dn, dn_in, fin, fin_in,
+    w_sem, s1, r1, s2, r2, s3, r3, s4, r4, s5, r5, s6, r6, s7, r7,
+    sa, ra, sb, rb, sc, rc_, sd, rd, s8, r8, s9, r9,
+):
+    side, row, col = (lax.axis_index(n) for n in ("side", "row", "col"))
+    his = cols // 2
+    core, hi = col % 2, col // 2
+    mate = hi * 2 + (1 - core)
+    half = cols // 2
+
+    def at(s, r, c):
+        return {"side": s, "row": r, "col": c}
+
+    def rcopy(src, dst, ss, rs, dev):
+        return pltpu.make_async_remote_copy(
+            src_ref=src, dst_ref=dst, send_sem=ss, recv_sem=rs, device_id=dev, device_id_type=MESH
+        )
+
+    def row_peer(d):
+        return lax.rem(row + d, rows)
+
+    def col_peer(d):
+        return lax.rem(col + d, cols)
+
+    def hi_peer(d):
+        return lax.rem(hi + d, his) * 2 + core
+
+    weights = [
+        pltpu.make_async_copy(h.at[0], w, w_sem.at[i])
+        for i, (h, w) in enumerate(
+            ((out_hbm, w_out), (gate_hbm, w_gate), (up_hbm, w_up), (down_hbm, w_down))
+        )
+    ]
+
+    @pl.when(side == 1)
+    def _():
+        for copy in weights:
+            copy.start()
+
+    barrier = pltpu.get_barrier_semaphore()
+
+    def greet(dev):
+        pl.semaphore_signal(barrier, inc=1, device_id=dev, device_id_type=MESH)
+
+    for d in range(rows):
+        greet(at(1 - side, row_peer(d), col))
+    for d in range(1, cols):
+        greet(at(1 - side, row, col_peer(d)))
+
+    @pl.when(side == 1)
+    def _():
+        for d in range(1, rows):
+            greet(at(1, row_peer(d), col))
+        for d in range(1, cols):
+            greet(at(1, row, col_peer(d)))
+        pl.semaphore_wait(barrier, 2 * (rows + cols) - 3)
+
+    @pl.when(side == 0)
+    def _():
+        pl.semaphore_wait(barrier, rows + cols - 1)
+
+    group = residual.shape[0] // rows
+    slots = group // cols
+    quarter = residual.shape[0] // cols
+    width = residual.shape[1]
+    heads = att.shape[2]
+
+    def head_copy(d):
+        return rcopy(att.at[row_peer(d)], xg.at[row, col], s1.at[d], r1.at[d], at(1, row_peer(d), col))
+
+    @pl.when(side == 0)
+    def _():
+        for d in range(rows):
+            head_copy(d).start()
+        for d in range(rows):
+            head_copy(d).wait_send()
+
+    @pl.when(side == 1)
+    def _():
+        for d in range(rows):
+            head_copy(d).wait_recv()
+        mine = xg.at[:, col]
+        own = rcopy(mine, mine, s2.at[0], r2.at[0], at(1, row, mate))
+        own.start()
+        across = [
+            rcopy(mine, mine, s2.at[d], r2.at[d], at(1, row, hi_peer(d))) for d in range(1, his)
+        ]
+        for copy in across:
+            copy.start()
+        passed = []
+        for d in range(1, his):
+            across[d - 1].wait_recv()
+            got = xg.at[:, hi_peer(his - d)]
+            copy = rcopy(got, got, s2.at[his + d - 1], r2.at[his + d - 1], at(1, row, mate))
+            copy.start()
+            passed.append(copy)
+        own.wait_recv()
+        for copy in passed:
+            copy.wait_recv()
+        total = rows * cols * slots
+        xf[...] = xg[...].astype(F32).reshape(total * heads, HD)
+        for h in range(heads):
+            xb[:, h * HD : (h + 1) * HD] = xf[pl.ds(h, total, stride=heads), :].astype(BF16)
+
+        tiles, tile = part.shape[0], part.shape[3]
+        weights[0].wait()
+
+        def proj_copy(j, d):
+            return rcopy(
+                part.at[j, row_peer(d)], rs_in.at[d - 1, j], s3.at[d - 1, j], r3.at[d - 1, j],
+                at(1, row_peer(d), col),
+            )
+
+        @pl.loop(0, tiles)
+        def _(j):
+            w = w_out[:, pl.ds(pl.multiple_of(j * tile, tile), tile)]
+            res = jnp.dot(xb[...], w, preferred_element_type=F32).astype(BF16)
+            part[j] = res.reshape(rows, group, tile)
+            for d in range(1, rows):
+                proj_copy(j, d).start()
+
+        squares = jnp.zeros((group, 1), F32)
+        my_rows = pl.ds(pl.multiple_of(row * group, group), group)
+        for j in range(tiles):
+            value = part[j, row].astype(F32)
+            for d in range(1, rows):
+                proj_copy(j, d).wait_recv()
+                value = value + rs_in[d - 1, j].astype(F32)
+            lanes = slice(j * tile, (j + 1) * tile)
+            value = value + residual[my_rows, lanes].astype(F32)
+            stream[:, lanes] = value
+            squares = squares + jnp.sum(value * value, axis=1, keepdims=True)
+            xs[row, :, lanes] = (value * gain[:, lanes].astype(F32)).astype(BF16)
+        sq_out[...] = jnp.broadcast_to(squares, sq_out.shape)
+
+        def stream_copy(d):
+            return rcopy(
+                xs.at[row], xs.at[row], s4.at[d - 1], r4.at[d - 1], at(1, row_peer(d), col)
+            )
+
+        def square_copy(d):
+            return rcopy(
+                sq_out, sq_in.at[d - 1], s5.at[d - 1], r5.at[d - 1], at(1, row, col_peer(d))
+            )
+
+        def inv_copy(d):
+            return rcopy(
+                inv_all.at[row], inv_all.at[row], s6.at[d - 1], r6.at[d - 1],
+                at(1, row_peer(d), col),
+            )
+
+        for d in range(1, cols):
+            square_copy(d).start()
+        for d in range(1, rows):
+            stream_copy(d).start()
+        sums = sq_out[...]
+        for d in range(1, cols):
+            square_copy(d).wait_recv()
+            sums = sums + sq_in[d - 1]
+        inv_all[row] = lax.rsqrt(sums / D + eps)
+        for d in range(1, rows):
+            inv_copy(d).start()
+        for d in range(1, rows):
+            stream_copy(d).wait_recv()
+        for d in range(1, rows):
+            inv_copy(d).wait_recv()
+        weights[1].wait()
+        weights[2].wait()
+        weights[3].wait()
+
+        steps, unit = gu.shape[0], gu.shape[5]
+
+        def core_copy(j):
+            return rcopy(gu.at[j, 1 - core], core_in.at[j], sa.at[j], ra.at[j], at(1, row, mate))
+
+        def x_copy(j, d):
+            there = lax.rem(hi + d, his)
+            return rcopy(
+                sum_out.at[j, there], x_in.at[d - 1, j], sb.at[d - 1, j], rb.at[d - 1, j],
+                at(1, row, hi_peer(d)),
+            )
+
+        def hid_copy(j, d):
+            dev = mate if d == 0 else hi_peer(d)
+            return rcopy(hid.at[j, col], hid.at[j, col], sc.at[d, j], rc_.at[d, j], at(1, row, dev))
+
+        def fwd_copy(j, d):
+            got = hid.at[j, hi_peer(his - d)]
+            return rcopy(got, got, sd.at[d - 1, j], rd.at[d - 1, j], at(1, row, mate))
+
+        acc[...] = jnp.zeros_like(acc)
+        lags = (0, 1, 3, 5, 6)
+
+        @pl.loop(0, steps + lags[4])
+        def _(i):
+            def stage(k):
+                j = i - lags[k]
+                return j, jnp.logical_and(j >= 0, j < steps)
+
+            j0, on0 = stage(0)
+
+            @pl.when(on0)
+            def _():
+                at_cols = pl.ds(pl.multiple_of(j0 * unit, unit), unit)
+                x = xs[...].reshape(rows * group, width)
+                scale = inv_all[...].reshape(rows * group, HD)[:, :1]
+                for n, w in enumerate((w_gate, w_up)):
+                    res = jnp.dot(x, w[:, at_cols], preferred_element_type=F32) * scale
+                    res = res.astype(BF16)
+                    for q in range(cols):
+                        gu[j0, q % 2, q // 2, n] = res[q * quarter : (q + 1) * quarter]
+                core_copy(j0).start()
+
+            j1, on1 = stage(1)
+
+            @pl.when(on1)
+            def _():
+                core_copy(j1).wait_recv()
+                sum_out[j1] = (gu[j1, core].astype(F32) + core_in[j1].astype(F32)).astype(BF16)
+                for d in range(1, his):
+                    x_copy(j1, d).start()
+
+            j2, on2 = stage(2)
+
+            @pl.when(on2)
+            def _():
+                both = sum_out[j2, hi].astype(F32)
+                for d in range(1, his):
+                    x_copy(j2, d).wait_recv()
+                    both = both + x_in[d - 1, j2].astype(F32)
+                gate, up = both[0], both[1]
+                hid[j2, col] = (gate / (1.0 + jnp.exp(-gate)) * up).astype(BF16)
+                for d in range(his):
+                    hid_copy(j2, d).start()
+
+            j3, on3 = stage(3)
+
+            @pl.when(on3)
+            def _():
+                for d in range(1, his):
+                    hid_copy(j3, d).wait_recv()
+                    fwd_copy(j3, d).start()
+
+            j4, on4 = stage(4)
+
+            @pl.when(on4)
+            def _():
+                hid_copy(j4, 0).wait_recv()
+                for d in range(1, his):
+                    fwd_copy(j4, d).wait_recv()
+                h = hid[j4].reshape(rows * group, unit)
+                w = w_down[pl.ds(pl.multiple_of(j4 * unit, unit), unit), :]
+                acc[...] += jnp.dot(h, w, preferred_element_type=F32)
+
+        dn[...] = acc[...].astype(BF16).reshape(rows, group, width)
+
+        def down_copy(d):
+            return rcopy(
+                dn.at[row_peer(d)], dn_in.at[d - 1], s7.at[d - 1], r7.at[d - 1],
+                at(1, row_peer(d), col),
+            )
+
+        for d in range(1, rows):
+            down_copy(d).start()
+        last = stream[...] + dn[row].astype(F32)
+        for d in range(1, rows):
+            down_copy(d).wait_recv()
+            last = last + dn_in[d - 1].astype(F32)
+        last = last.astype(BF16).astype(F32)
+        for c in range(cols):
+            fin[c] = last[c * slots : (c + 1) * slots].astype(BF16)
+
+        own.wait_send()
+        for copy in across + passed:
+            copy.wait_send()
+        for d in range(1, rows):
+            @pl.loop(0, tiles)
+            def _(j):
+                proj_copy(j, d).wait_send()
+            stream_copy(d).wait_send()
+            inv_copy(d).wait_send()
+            down_copy(d).wait_send()
+        for d in range(1, cols):
+            square_copy(d).wait_send()
+
+        @pl.loop(0, steps)
+        def _(j):
+            core_copy(j).wait_send()
+            for d in range(his):
+                hid_copy(j, d).wait_send()
+            for d in range(1, his):
+                x_copy(j, d).wait_send()
+                fwd_copy(j, d).wait_send()
+
+    def up_copy(d):
+        return rcopy(
+            fin.at[col_peer(d)], fin_in.at[col - half], s8.at[d - 1], r8.at[col - half],
+            at(1, row, col_peer(d)),
+        )
+
+    def low_copy(d):
+        return rcopy(
+            fin.at[col_peer(d)], fin_in.at[col], s9.at[d], r8.at[col], at(0, row, col_peer(d))
+        )
+
+    @pl.when(side == 1)
+    def _():
+        @pl.when(col >= half)
+        def _():
+            for d in range(1, cols):
+                up_copy(d).start()
+            fin_in[col - half] = fin[col]
+            for d in range(1, cols):
+                up_copy(d).wait_send()
+
+        @pl.when(col < half)
+        def _():
+            for d in range(cols):
+                low_copy(d).start()
+            for d in range(cols):
+                low_copy(d).wait_send()
+
+    for k in range(half):
+        @pl.when(jnp.logical_or(side == 0, col != half + k))
+        def _():
+            rcopy(
+                fin.at[0], fin_in.at[k], s9.at[0], r8.at[k], at(1 - side, row, col)
+            ).wait_recv()
+        out[:, k * width : (k + 1) * width] = fin_in[k]
+
+
+def layer(rows, cols, att, residual, gain, out_w, gate_w, up_w, down_w):
+    _, slots, heads, _ = att.shape
+    total, width = residual.shape
+    group, quarter, his = total // rows, total // cols, cols // 2
+    ff = gate_w.shape[2]
+    tile, unit = tile_of(width), tile_of(ff)
+    tiles, steps = width // tile, ff // unit
+    dma = pltpu.SemaphoreType.DMA
+    vmem = pltpu.VMEM
+    scratch = [
+        vmem(out_w.shape[1:], BF16),
+        vmem(gate_w.shape[1:], BF16),
+        vmem(up_w.shape[1:], BF16),
+        vmem(down_w.shape[1:], BF16),
+        vmem((rows, cols, slots, heads, HD), BF16),
+        vmem((total * heads, HD), F32),
+        vmem((total, heads * HD), BF16),
+        vmem((tiles, rows, group, tile), BF16),
+        vmem((rows - 1, tiles, group, tile), BF16),
+        vmem((group, width), F32),
+        vmem((group, HD), F32),
+        vmem((cols - 1, group, HD), F32),
+        vmem((rows, group, HD), F32),
+        vmem((rows, group, width), BF16),
+        vmem((steps, 2, his, 2, quarter, unit), BF16),
+        vmem((steps, his, 2, quarter, unit), BF16),
+        vmem((steps, his, 2, quarter, unit), BF16),
+        vmem((his - 1, steps, 2, quarter, unit), BF16),
+        vmem((steps, cols, quarter, unit), BF16),
+        vmem((total, width), F32),
+        vmem((rows, group, width), BF16),
+        vmem((rows - 1, group, width), BF16),
+        vmem((cols, slots, width), BF16),
+        vmem((cols // 2, slots, width), BF16),
+        dma((4,)),
+        dma((rows,)), dma((rows,)),
+        dma((2 * his - 1,)), dma((2 * his - 1,)),
+        dma((rows - 1, tiles)), dma((rows - 1, tiles)),
+        dma((rows - 1,)), dma((rows - 1,)),
+        dma((cols - 1,)), dma((cols - 1,)),
+        dma((rows - 1,)), dma((rows - 1,)),
+        dma((rows - 1,)), dma((rows - 1,)),
+        dma((steps,)), dma((steps,)),
+        dma((his - 1, steps)), dma((his - 1, steps)),
+        dma((his, steps)), dma((his, steps)),
+        dma((his - 1, steps)), dma((his - 1, steps)),
+        dma((cols,)), dma((cols // 2,)),
+        dma((cols,)), dma((1,)),
+    ]
+    in_vmem = pl.BlockSpec(memory_space=pltpu.VMEM)
+    anywhere = pl.BlockSpec(memory_space=pl.ANY)
+
+    def kernel(*refs):
+        layer_kernel(rows, cols, *refs)
+
+    weight_bytes = 2 * (out_w.size + gate_w.size + up_w.size + down_w.size)
+    return pl.pallas_call(
+        kernel,
+        out_shape=jax.ShapeDtypeStruct((slots, width * cols // 2), BF16),
+        in_specs=[in_vmem] * 3 + [anywhere] * 4,
+        out_specs=in_vmem,
+        scratch_shapes=scratch,
+        compiler_params=pltpu.CompilerParams(
+            collective_id=0, has_side_effects=True, vmem_limit_bytes=62 * 1024 * 1024
+        ),
+        cost_estimate=pl.CostEstimate(
+            flops=total * weight_bytes, bytes_accessed=weight_bytes, transcendentals=0
+        ),
+        name="layer",
+    )(att, residual, gain, out_w, gate_w, up_w, down_w)
+
+
 def local(
     queries,
     new_entries,
@@ -96,51 +508,14 @@
     down_weight,
 ):
     attended = attention(queries, new_entries, cache_keys[0], cache_values[0], lengths)
-    slot_count = attended.shape[0]
-    row_count = lax.axis_size("row")
-    col_count = lax.axis_size("col")
-    head_block = attended.shape[1] // row_count
-    split_heads = attended.reshape(slot_count, row_count, head_block)
-    moved = from_behind(split_heads, "side", 1)
-    blocks = lax.all_to_all(moved, "row", split_axis=1, concat_axis=0, tiled=True)
-    sectioned = blocks.reshape(row_count, 1, slot_count, head_block)
-    out_block = out_weight[0]
-    partial_value = jnp.einsum(
-        "akjd,de->akje",
-        lax.all_gather(sectioned, "col", axis=1, tiled=True),
-        out_block,
-        preferred_element_type=jnp.float32,
+    slots = attended.shape[0]
+    rows = lax.axis_size("row")
+    cols = lax.axis_size("col")
+    att = attended.reshape(slots, rows, H // rows, HD).transpose(1, 0, 2, 3)
+    return layer(
+        rows, cols, att, residual, norm_gain[None, :],
+        out_weight, gate_weight, up_weight, down_weight,
     )
-    col_width = out_block.shape[1]
-    total_rows = row_count * col_count * slot_count
-    projected = lax.psum(
-        partial_value.reshape(total_rows, col_width).astype(jnp.bfloat16), "row"
-    ).astype(jnp.float32)
-    stream = residual.astype(jnp.float32) + projected
-    squares = lax.psum(jnp.sum(stream * stream, axis=1), "col")
-    inv_rms = lax.rsqrt(squares / D + eps)
-    normed = (stream * inv_rms[:, None] * norm_gain.astype(jnp.float32)[None, :]).astype(
-        jnp.bfloat16
-    )
-    gate_block = gate_weight[0]
-    up_block = up_weight[0]
-    down_block = down_weight[0]
-    gate_part = jnp.dot(normed, gate_block, preferred_element_type=jnp.float32)
-    up_part = jnp.dot(normed, up_block, preferred_element_type=jnp.float32)
-    gate_total, up_total = (
-        lax.psum(gate_part.astype(jnp.bfloat16), "col").astype(jnp.float32),
-        lax.psum(up_part.astype(jnp.bfloat16), "col").astype(jnp.float32),
-    )
-    hidden = (jax.nn.silu(gate_total) * up_total).astype(jnp.bfloat16)
-    down_part = jnp.dot(hidden, down_block, preferred_element_type=jnp.float32)
-    down_total = lax.psum(down_part.astype(jnp.bfloat16), "row").astype(jnp.float32)
-    final = (stream + down_total).astype(jnp.bfloat16)
-    group_rows = col_count * slot_count
-    mine_rows = lax.dynamic_slice_in_dim(final, lax.axis_index("row") * group_rows, group_rows, 0)
-    slot_rows = lax.all_to_all(mine_rows, "col", split_axis=0, concat_axis=1, tiled=True)
-    half_width = slot_rows.shape[1] // 2
-    returned = from_behind(slot_rows[:, :half_width], "side", -1)
-    return jnp.where(lax.axis_index("side") == 0, returned, slot_rows[:, half_width:])
 
 
 def solution(mesh):

time: 220 us -> 86.3 us (0.39)
  waiting for transfers between devices: 112 us -> 0 us
  Pallas kernels: 0 us -> 59.9 us
  matrix products: 34.1 us -> 2 us
  blocking collectives: 28.7 us -> 0 us
  between operations: 13.3 us -> 0.15 us
  starting transfers between devices: 6.25 us -> 0 us
  other arithmetic: 11.9 us -> 8.61 us
  local copies, waits for them, and re-layouts: 13.1 us -> 15.4 us
    psum x3 -> x0, waiting for transfers between devices: 106 us -> none  [the longest x1 35.7 us: local(): lax.psum(down_part.astype(jnp.bfloat16), 'row').astype(jnp.float32)]
    pallas_call x0 -> x1, Pallas kernels: none -> 59.9 us  [layer(): pl.pallas_call(kernel, out_shape=jax.ShapeDtypeStruct((slots, width * col...]
    dot_general x4 -> x0, matrix products: 32.1 us -> none  [the longest x1 8.84 us: local(): down_part = jnp.dot(hidden, down_block, preferred_element_type=jnp.float32)]
    all_to_all x2 -> x0, blocking collectives: 17.1 us -> none  [the longest x1 10.4 us: local(): lax.all_to_all(moved, 'row', split_axis=1, concat_axis=0, tiled=True)]
    ppermute x2 -> x0, waiting for transfers between devices: 6.39 us -> none  [from_behind(): lax.ppermute(value, axis, [(source, source + steps) for source in range(f...]
    ppermute x2 -> x0, starting transfers between devices: 6.17 us -> none  [from_behind(): lax.ppermute(value, axis, [(source, source + steps) for source in range(f...]
    psum x1 -> x0, blocking collectives: 5.85 us -> none  [local(): squares = lax.psum(jnp.sum(stream * stream, axis=1), 'col')]
    all_gather x1 -> x0, blocking collectives: 5.79 us -> none  [local(): lax.all_gather(sectioned, 'col', axis=1, tiled=True)]
  transfers between devices with their start and end apart: 5 -> 0, of which waited for: 5 -> 0; matrix products, arithmetic and copies ran while one was open for 0% -> 0% of each run, Pallas kernels for 0% -> 0%
where the time goes in v1:
time: 86.3 us; the launch traced here: 86 us
  Pallas kernels  59.9 us (69%)
  local copies, waits for them, and re-layouts  15.4 us (18%)
  other arithmetic  8.61 us (10%)
  matrix products  2 us (2%)
    pallas_call x1, Pallas kernels, layer(): pl.pallas_call(kernel, out_shape=jax.ShapeDtypeStruct((slots, width * col...  59.9 us
    unnamed x18, local copies, waits for them, and re-layouts  11.6 us
    another operation x2, other arithmetic  4.77 us
    slice x1, local copies, waits for them, and re-layouts, rotary(): second = vec[..., half:]  2.53 us
    cos x2, other arithmetic, rotary(): cosine = jnp.cos(angles)  2 us

profile of v1, /device:TPU:0, one launch (start us, length us, event | category | flops | bytes accessed | tf_op | source)
XLA Modules:
  0.0 86.0 jit_solution(2219481392713738127)
XLA Ops:
  0.0 0.7 convert_element_type.42
  0.7 0.7 multiply_add_fusion
  1.3 0.1 multiply_cosine_fusion.1
  1.5 1.9 %multiply_cosine_fusion = (f32[4,256,64]{2,1,0:T(8,128)S(1)}, f32[4,256,64]{2,1,0:T(8,128)S(1)}) fusion(f32[4,64]{1,0:T(4,128)S(1)} %get-tuple-element.21, f32[256]{0:T(256)S(1)} %iota_convert_fusion), kind=kLoop, calls=%fused_computation.13 | loop fusion | flops 65536 | bytes 526336 | tf_op jit(solution)/shard_map/cos | solution.py:32
  3.4 2.9 %copy.13 = bf16[1,4,256,1024]{2,3,1,0:T(8,128)(2,1)S(1)} copy(bf16[1,4,256,1024]{3,2,1,0:T(8,128)(2,1)} %param.13) | data formatting | bytes 4194304 | tf_op args[2]
  6.2 2.5 %fusion.32 = (f32[4,256,8,64]{1,3,2,0:T(8,128)}, f32[4,256,8,64]{1,3,2,0:T(8,128)}) fusion(bf16[4,256,8,128]{1,3,2,0:T(8,128)(2,1)S(1)} %bitcast.35), kind=kLoop, calls=%fused_computation.51 | loop fusion | bytes 8388608 | tf_op jit(solution)/shard_map/slice | solution.py:31
  8.7 0.0 copy-start
  8.7 3.9 %copy.20 = f32[4,256,8,64]{3,1,2,0:T(8,128)} copy(f32[4,256,8,64]{1,3,2,0:T(8,128)} %get-tuple-element.10) | data formatting | bytes 4194304
  12.7 0.0 copy-done
  12.7 2.7 %copy.21 = f32[4,256,8,64]{3,1,2,0:T(8,128)} copy(f32[4,256,8,64]{1,3,2,0:T(8,128)S(1)} %copy-done) | data formatting | bytes 4194304
  15.4 0.0 copy-start.2
  15.4 0.0 copy-start.5
  15.4 4.7 %subtract_convert_fusion = (bf16[4,256,8,64]{3,1,2,0:T(8,128)(2,1)S(1)}, bf16[4,256,8,64]{3,1,2,0:T(8,128)(2,1)S(1)}) fusion(f32[4,256,8,64]{3,1,2,0:T(8,128)} %copy.21, f32[4,256,8,64]{3,1,2,0:T(8,128)} %copy.20, f32[4,256,64]{2,1,0:T(8,128)S(1)} %get-tuple-element.18, f32[4,256,64]{2,1,0:T(8,128)S(1)} %get-tuple-element.17), kind=kLoop, calls=%fused_computation.1 | loop fusion | flops 4194304 | bytes 6815744 | tf_op jit(solution)/shard_map/convert.6
  20.1 0.0 copy-done.2
  20.2 0.1 fusion.24
  20.3 0.0 copy-done.5
  20.3 0.1 iota_compare_fusion
  20.4 0.0 copy-start.3
  20.4 0.0 copy-start.1
  20.4 1.3 %select_reduce_fusion = (f32[4,8,8]{2,1,0:T(8,128)S(1)}, f32[4,8,8,256]{3,2,1,0:T(8,128)S(1)}) fusion(pred[4,256]{1,0:T(4,128)(4,1)S(1)} %iota_compare_fusion, bf16[4,256,8,64]{3,1,2,0:T(8,128)(2,1)S(1)} %get-tuple-element.8, bf16[4,256,8,64]{3,1,2,0:T(8,128)(2,1)S(1)} %get-tuple-element.7, bf16[4,8,8,64]{3,2,1,0:T(8,128)(2,1)S(1)} %get-tuple-element.12, ...), kind=kOutput, calls=%fused_computation.15 | convolution fusion | flops 21298944 | bytes 2426880 | tf_op jit(solution)/shard_map/sgqd,scgd->sgqc/dot_general | solution.py:58
  21.7 0.0 copy-done.3
  21.7 0.1 subtract_convert_fusion.2
  21.8 0.1 maximum_bitcast_fusion
  21.9 0.2 fusion.26
  22.1 0.2 fusion.18
  22.4 0.0 copy-done.1
  22.4 0.6 copy.24
  23.0 0.0 copy-start.4
  23.0 0.4 fusion.15
  23.5 0.6 copy_bitcast_fusion.1.refs_0_
  24.1 0.0 copy-done.4
  24.1 0.6 broadcast_in_dim.38.refs_2_
  24.7 59.9 %layer.1 = bf16[4,4096]{1,0:T(4,128)(2,1)} custom-call(bf16[4,4,16,128]{3,2,1,0:T(8,128)(2,1)} %copy_bitcast_fusion.1.refs_0_, bf16[64,2048]{1,0:T(8,128)(2,1)} %refs_1_.1, bf16[1,2048]{1,0:T(2,128)(2,1)} %broadcast_in_dim.38.refs_2_, bf16[1,2048,2048]{2,1,0:T(8,128)(2,1)} %refs_3_.1, bf16[1,2048,3584]{2,1,0:T(8,128)(2,1)} %refs_4_.1, ...), custom_call_target="tpu_custom_call" | custom-call | flops 3355443200 | bytes 52428800 | tf_op jit(solution)/shard_map/layer/pallas_call | solution.py:481
  84.6 1.4 %copy.42 = bf16[4,4096]{1,0:T(4,128)(2,1)} copy(bf16[4,4096]{1,0:T(4,128)(2,1)} %layer.1) | data formatting | bytes 65536
  (8 shorter events, 0.1 us)
Async XLA Ops:
  8.7 3.9 %copy-start = (f32[4,256,8,64]{1,3,2,0:T(8,128)S(1)}, f32[4,256,8,64]{1,3,2,0:T(8,128)}, u32[]{:S(2)}) copy-start(f32[4,256,8,64]{1,3,2,0:T(8,128)} %get-tuple-element.9) | copy-start | bytes 6291460
  15.4 4.7 %copy-start.2 = (bf16[4,8192]{1,0:T(4,128)(2,1)S(1)}, bf16[4,8192]{1,0:T(4,128)(2,1)}, u32[]{:S(2)}) copy-start(bf16[4,8192]{1,0:T(4,128)(2,1)} %param.11) | copy-start | bytes 196612
  15.4 4.9 %copy-start.5 = (s32[4]{0:T(128)S(1)}, s32[4]{0:T(128)}, u32[]{:S(2)}) copy-start(s32[4]{0:T(128)} %param.15) | copy-start | bytes 52
  20.4 1.3 %copy-start.3 = (bf16[4,2048]{1,0:T(4,128)(2,1)S(1)}, bf16[4,2048]{1,0:T(4,128)(2,1)}, u32[]{:S(2)}) copy-start(bf16[4,2048]{1,0:T(4,128)(2,1)} %param.12) | copy-start | bytes 49156
  20.4 2.0 %copy-start.1 = (bf16[1,4,256,1024]{3,2,1,0:T(8,128)(2,1)S(1)}, bf16[1,4,256,1024]{3,2,1,0:T(8,128)(2,1)}, u32[]{:S(2)}) copy-start(bf16[1,4,256,1024]{3,2,1,0:T(8,128)(2,1)} %param.14) | copy-start | bytes 6291460
  23.0 1.1 %copy-start.4 = (bf16[2048]{0:T(1024)(128)(2,1)S(1)}, bf16[2048]{0:T(1024)(128)(2,1)}, u32[]{:S(2)}) copy-start(bf16[2048]{0:T(1024)(128)(2,1)} %param.17) | copy-start | bytes 12292

commit v2 on v1

--- a/solution.py
+++ b/solution.py
@@ -17,67 +17,6 @@
 eps = 1e-05
 
 
-def frequencies(lengths):
-    seq = lengths.astype(jnp.float32) + 1.0
-    stretch = jnp.maximum(stretch_factor * seq / ORIG - (stretch_factor - 1.0), 1.0)
-    log_base = jnp.log(jnp.float32(rope_theta)) + HD / (HD - 2.0) * jnp.log(stretch)
-    expo = jnp.arange(HD // 2).astype(jnp.float32) * (2.0 / HD)
-    return jnp.exp(-expo[None, :] * log_base[:, None])
-
-
-def rotary(vec, angles):
-    half = vec.shape[-1] // 2
-    first = vec[..., :half]
-    second = vec[..., half:]
-    cosine = jnp.cos(angles)
-    sine = jnp.sin(angles)
-    return jnp.concatenate(
-        [first * cosine - second * sine, second * cosine + first * sine], axis=-1
-    )
-
-
-def attention(queries, new_entries, keys, values, lengths):
-    slots = queries.shape[0]
-    span = keys.shape[1]
-    per_group = H // KVH
-    freqs = frequencies(lengths)
-    angle_new = lengths.astype(jnp.float32)[:, None] * freqs
-    angle_cache = jnp.arange(span).astype(jnp.float32)[None, :, None] * freqs[:, None, :]
-    query_rot = rotary(
-        queries.astype(jnp.float32).reshape(slots, H, HD), angle_new[:, None, :]
-    ).astype(jnp.bfloat16)
-    query_rot = query_rot.reshape(slots, KVH, per_group, HD)
-    key_fresh = new_entries[:, : KVH * HD].astype(jnp.float32).reshape(slots, KVH, HD)
-    value_fresh = new_entries[:, KVH * HD :].astype(jnp.float32).reshape(slots, KVH, HD)
-    key_new_rot = rotary(key_fresh, angle_new[:, None, :]).astype(jnp.bfloat16)
-    key_rot = rotary(
-        keys.astype(jnp.float32).reshape(slots, span, KVH, HD), angle_cache[:, :, None, :]
-    ).astype(jnp.bfloat16)
-    scale = HD ** (-0.5)
-    scores = (
-        jnp.einsum("sgqd,scgd->sgqc", query_rot, key_rot, preferred_element_type=jnp.float32)
-        * scale
-    )
-    own_score = (
-        jnp.einsum("sgqd,sgd->sgq", query_rot, key_new_rot, preferred_element_type=jnp.float32)
-        * scale
-    )
-    valid_mask = (jnp.arange(span)[None, :] < lengths[:, None])[:, None, None, :]
-    highest = jnp.maximum(jnp.max(jnp.where(valid_mask, scores, -1e30), axis=-1), own_score)
-    weights = jnp.where(valid_mask, jnp.exp(scores - highest[..., None]), 0.0)
-    own_weight = jnp.exp(own_score - highest)
-    totals = jnp.sum(weights, axis=-1) + own_weight
-    weights16 = weights.astype(jnp.bfloat16)
-    mixed = jnp.einsum(
-        "sgqc,scgd->sgqd",
-        weights16,
-        values.reshape(slots, span, KVH, HD),
-        preferred_element_type=jnp.float32,
-    )
-    mixed = mixed + own_weight[..., None] * value_fresh[:, :, None, :]
-    return (mixed / totals[..., None]).reshape(slots, H * HD).astype(jnp.bfloat16)
-
-
 MESH = pl.DeviceIdType.MESH
 F32 = jnp.float32
 BF16 = jnp.bfloat16
@@ -87,12 +26,100 @@
     return next(t for t in (512, 256, 128) if width % t == 0)
 
 
+def attention(
+    rows, queries, entries, lengths, keys, values, qf, ef, att, key_hbm, value_hbm, c_sem, head_copy
+):
+    slots, span, _ = keys.shape
+    per_group = H // KVH
+    heads = H // rows
+    for s in range(slots):
+        for h in range(H):
+            qf[s, h : h + 1, :] = queries[s : s + 1, h * HD : (h + 1) * HD].astype(F32)
+        for h in range(2 * KVH):
+            ef[s, h : h + 1, :] = entries[s : s + 1, h * HD : (h + 1) * HD].astype(F32)
+    lane = lax.broadcasted_iota(jnp.int32, (1, HD), 1)
+    lower = lane < HD // 2
+    expo = jnp.where(lower, lane, lane - HD // 2).astype(F32) * (2.0 / HD)
+    fine = 16
+    step = lax.broadcasted_iota(jnp.int32, (fine, HD), 0).astype(F32)
+    place = lax.broadcasted_iota(jnp.int32, (H, span), 1)
+    scale = HD ** (-0.5)
+
+    def rot(vec, cosine, sine):
+        return vec * cosine + pltpu.roll(vec, HD // 2, 1) * sine
+
+    def rounded(vec):
+        return vec.astype(BF16).astype(F32)
+
+    @pl.loop(0, slots)
+    def _(s):
+        length = jnp.full((1, HD), lengths[s], jnp.int32).astype(F32)
+        stretch = jnp.maximum(stretch_factor * (length + 1.0) / ORIG - (stretch_factor - 1.0), 1.0)
+        log_base = jnp.log(jnp.full((1, HD), rope_theta, F32)) + HD / (HD - 2.0) * jnp.log(stretch)
+        freq = jnp.exp(-expo * log_base)
+        cos_new = jnp.cos(length * freq)
+        sin_new = jnp.sin(length * freq)
+        sin_new = jnp.where(lower, -sin_new, sin_new)
+        cos_b, sin_b = jnp.cos(step * freq), jnp.sin(step * freq)
+        cos_a, sin_a = jnp.cos(step * (fine * freq)), jnp.sin(step * (fine * freq))
+        sign = jnp.where(lower, -1.0, 1.0)
+        sin_b_signed, cos_b_signed = sin_b * sign, cos_b * sign
+        cos_t, sin_t = [], []
+        for a in range(span // fine):
+            ca, sa = cos_a[a : a + 1], sin_a[a : a + 1]
+            cos_t.append(ca * cos_b - sa * sin_b)
+            sin_t.append(sa * cos_b_signed + ca * sin_b_signed)
+        cos_t = jnp.concatenate(cos_t, axis=0)
+        sin_t = jnp.concatenate(sin_t, axis=0)
+
+        q = rounded(rot(qf[s], cos_new, sin_new))
+        new = ef[s]
+        key_new = rounded(rot(new[:KVH], cos_new, sin_new))
+        value_new = new[KVH:]
+        pltpu.make_async_copy(key_hbm.at[0, s], keys.at[s], c_sem.at[0, s]).wait()
+        scores, own = [], []
+        for g in range(KVH):
+            q_g = q[g * per_group : (g + 1) * per_group]
+            key = keys[s, :, g * HD : (g + 1) * HD].astype(F32)
+            key = rot(key, cos_t, sin_t).astype(BF16)
+            scores.append(
+                lax.dot_general(
+                    q_g.astype(BF16), key, (((1,), (1,)), ((), ())), preferred_element_type=F32
+                )
+            )
+            own.append(jnp.sum(q_g * key_new[g : g + 1], axis=1, keepdims=True))
+        scores = jnp.concatenate(scores, axis=0) * scale
+        own = jnp.concatenate(own, axis=0) * scale
+        valid = place < jnp.full((H, span), lengths[s], jnp.int32)
+        top = jnp.maximum(jnp.max(jnp.where(valid, scores, -1e30), axis=1, keepdims=True), own)
+        weight = jnp.where(valid, jnp.exp(scores - top), 0.0)
+        own_weight = jnp.exp(own - top)
+        total = jnp.sum(weight, axis=1, keepdims=True) + own_weight
+        pltpu.make_async_copy(value_hbm.at[0, s], values.at[s], c_sem.at[1, s]).wait()
+        mixed = []
+        for g in range(KVH):
+            part = slice(g * per_group, (g + 1) * per_group)
+            value = values[s, :, g * HD : (g + 1) * HD]
+            res = jnp.dot(weight[part].astype(BF16), value, preferred_element_type=F32)
+            mixed.append(res + own_weight[part] * value_new[g : g + 1])
+        attended = jnp.concatenate(mixed, axis=0) / total
+        for r in range(rows):
+            att[r, s] = attended[r * heads : (r + 1) * heads].astype(BF16)
+        for d in range(rows):
+            head_copy(s, d).start()
+
+    for s in range(slots):
+        for d in range(rows):
+            head_copy(s, d).wait_send()
+
+
 def layer_kernel(
-    rows, cols, att, residual, gain, out_hbm, gate_hbm, up_hbm, down_hbm, out,
-    w_out, w_gate, w_up, w_down,
+    rows, cols, queries, entries, lengths, residual, gain, key_hbm, value_hbm,
+    out_hbm, gate_hbm, up_hbm, down_hbm, out,
+    w_out, w_gate, w_up, w_down, keys, values, qf, ef, att,
     xg, xf, xb, part, rs_in, stream, sq_out, sq_in, inv_all, xs,
     gu, core_in, sum_out, x_in, hid, acc, dn, dn_in, fin, fin_in,
-    w_sem, s1, r1, s2, r2, s3, r3, s4, r4, s5, r5, s6, r6, s7, r7,
+    w_sem, c_sem, s1, r1, s2, r2, s3, r3, s4, r4, s5, r5, s6, r6, s7, r7,
     sa, ra, sb, rb, sc, rc_, sd, rd, s8, r8, s9, r9,
 ):
     side, row, col = (lax.axis_index(n) for n in ("side", "row", "col"))
@@ -127,7 +154,17 @@
 
     @pl.when(side == 1)
     def _():
-        for copy in weights:
+        weights[0].start()
+
+    caches = [
+        pltpu.make_async_copy(h.at[0, s], v.at[s], c_sem.at[i, s])
+        for s in range(keys.shape[0])
+        for i, (h, v) in enumerate(((key_hbm, keys), (value_hbm, values)))
+    ]
+
+    @pl.when(side == 0)
+    def _():
+        for copy in caches:
             copy.start()
 
     barrier = pltpu.get_barrier_semaphore()
@@ -158,20 +195,24 @@
     width = residual.shape[1]
     heads = att.shape[2]
 
-    def head_copy(d):
-        return rcopy(att.at[row_peer(d)], xg.at[row, col], s1.at[d], r1.at[d], at(1, row_peer(d), col))
+    def head_copy(s, d):
+        to = row_peer(d)
+        return rcopy(
+            att.at[to, s], xg.at[row, col, s], s1.at[s, d], r1.at[s, d], at(1, to, col)
+        )
 
     @pl.when(side == 0)
     def _():
-        for d in range(rows):
-            head_copy(d).start()
-        for d in range(rows):
-            head_copy(d).wait_send()
+        attention(rows, queries, entries, lengths, keys, values, qf, ef, att, key_hbm, value_hbm, c_sem, head_copy)
 
     @pl.when(side == 1)
     def _():
-        for d in range(rows):
-            head_copy(d).wait_recv()
+        weights[0].wait()
+        for copy in weights[1:]:
+            copy.start()
+        for s in range(slots):
+            for d in range(rows):
+                head_copy(s, d).wait_recv()
         mine = xg.at[:, col]
         own = rcopy(mine, mine, s2.at[0], r2.at[0], at(1, row, mate))
         own.start()
@@ -196,7 +237,6 @@
             xb[:, h * HD : (h + 1) * HD] = xf[pl.ds(h, total, stride=heads), :].astype(BF16)
 
         tiles, tile = part.shape[0], part.shape[3]
-        weights[0].wait()
 
         def proj_copy(j, d):
             return rcopy(
@@ -223,7 +263,7 @@
             value = value + residual[my_rows, lanes].astype(F32)
             stream[:, lanes] = value
             squares = squares + jnp.sum(value * value, axis=1, keepdims=True)
-            xs[row, :, lanes] = (value * gain[:, lanes].astype(F32)).astype(BF16)
+            xs[row, :, lanes] = (value * gain[lanes].astype(F32)[None, :]).astype(BF16)
         sq_out[...] = jnp.broadcast_to(squares, sq_out.shape)
 
         def stream_copy(d):
@@ -422,8 +462,9 @@
         out[:, k * width : (k + 1) * width] = fin_in[k]
 
 
-def layer(rows, cols, att, residual, gain, out_w, gate_w, up_w, down_w):
-    _, slots, heads, _ = att.shape
+def layer(rows, cols, queries, entries, lengths, residual, gain, keys, values, out_w, gate_w, up_w, down_w):
+    slots = queries.shape[0]
+    heads = H // rows
     total, width = residual.shape
     group, quarter, his = total // rows, total // cols, cols // 2
     ff = gate_w.shape[2]
@@ -436,6 +477,11 @@
         vmem(gate_w.shape[1:], BF16),
         vmem(up_w.shape[1:], BF16),
         vmem(down_w.shape[1:], BF16),
+        vmem(keys.shape[1:], BF16),
+        vmem(values.shape[1:], BF16),
+        vmem((slots, H, HD), F32),
+        vmem((slots, 2 * KVH, HD), F32),
+        vmem((rows, slots, heads, HD), BF16),
         vmem((rows, cols, slots, heads, HD), BF16),
         vmem((total * heads, HD), F32),
         vmem((total, heads * HD), BF16),
@@ -456,8 +502,8 @@
         vmem((rows - 1, group, width), BF16),
         vmem((cols, slots, width), BF16),
         vmem((cols // 2, slots, width), BF16),
-        dma((4,)),
-        dma((rows,)), dma((rows,)),
+        dma((4,)), dma((2, slots)),
+        dma((slots, rows)), dma((slots, rows)),
         dma((2 * his - 1,)), dma((2 * his - 1,)),
         dma((rows - 1, tiles)), dma((rows - 1, tiles)),
         dma((rows - 1,)), dma((rows - 1,)),
@@ -481,17 +527,18 @@
     return pl.pallas_call(
         kernel,
         out_shape=jax.ShapeDtypeStruct((slots, width * cols // 2), BF16),
-        in_specs=[in_vmem] * 3 + [anywhere] * 4,
+        in_specs=[in_vmem, in_vmem, pl.BlockSpec(memory_space=pltpu.SMEM), in_vmem, in_vmem]
+        + [anywhere] * 6,
         out_specs=in_vmem,
         scratch_shapes=scratch,
         compiler_params=pltpu.CompilerParams(
-            collective_id=0, has_side_effects=True, vmem_limit_bytes=62 * 1024 * 1024
+            collective_id=0, has_side_effects=True, vmem_limit_bytes=63 * 1024 * 1024
         ),
         cost_estimate=pl.CostEstimate(
             flops=total * weight_bytes, bytes_accessed=weight_bytes, transcendentals=0
         ),
         name="layer",
-    )(att, residual, gain, out_w, gate_w, up_w, down_w)
+    )(queries, entries, lengths, residual, gain, keys, values, out_w, gate_w, up_w, down_w)
 
 
 def local(
@@ -507,14 +554,9 @@
     up_weight,
     down_weight,
 ):
-    attended = attention(queries, new_entries, cache_keys[0], cache_values[0], lengths)
-    slots = attended.shape[0]
-    rows = lax.axis_size("row")
-    cols = lax.axis_size("col")
-    att = attended.reshape(slots, rows, H // rows, HD).transpose(1, 0, 2, 3)
     return layer(
-        rows, cols, att, residual, norm_gain[None, :],
-        out_weight, gate_weight, up_weight, down_weight,
+        lax.axis_size("row"), lax.axis_size("col"), queries, new_entries, lengths, residual,
+        norm_gain, cache_keys, cache_values, out_weight, gate_weight, up_weight, down_weight,
     )
 
 

time: 86.3 us -> 65.4 us (0.76)
  local copies, waits for them, and re-layouts: 15.4 us -> 1.39 us
  other arithmetic: 8.61 us -> 0 us
  Pallas kernels: 59.9 us -> 63.8 us
  matrix products: 2 us -> 0 us
    unnamed x18 -> x1, local copies, waits for them, and re-layouts: 11.6 us -> 1.39 us
    another operation x2 -> x0, other arithmetic: 4.77 us -> none
    pallas_call x1, Pallas kernels: 59.9 us -> 63.8 us  [layer(): pl.pallas_call(kernel, out_shape=jax.ShapeDtypeStruct((slots, width * col...]
    slice x1 -> x0, local copies, waits for them, and re-layouts: 2.53 us -> none  [rotary(): second = vec[..., half:]]
    dot_general x3 -> x0, matrix products: 2 us -> none  [the longest x1 1.34 us: attention(): jnp.einsum('sgqd,scgd->sgqc', query_rot, key_rot, preferred_element_type=...]
    cos x2 -> x0, other arithmetic: 2 us -> none  [rotary(): cosine = jnp.cos(angles)]
where the time goes in v2:
time: 65.4 us; the launch traced here: 65.2 us
  Pallas kernels  63.8 us (98%)
  local copies, waits for them, and re-layouts  1.39 us (2%)
    pallas_call x1, Pallas kernels, layer(): pl.pallas_call(kernel, out_shape=jax.ShapeDtypeStruct((slots, width * col...  63.8 us
    unnamed x1, local copies, waits for them, and re-layouts  1.39 us

profile of v2, /device:TPU:0, one launch (start us, length us, event | category | flops | bytes accessed | tf_op | source)
XLA Modules:
  0.0 65.2 jit_solution(9621757829830163503)
XLA Ops:
  0.0 63.8 %layer.1 = bf16[4,4096]{1,0:T(4,128)(2,1)} custom-call(bf16[4,8192]{1,0:T(4,128)(2,1)} %refs_0_.1, bf16[4,2048]{1,0:T(4,128)(2,1)} %refs_1_.1, s32[4]{0:T(128)} %refs_2_.1, bf16[64,2048]{1,0:T(8,128)(2,1)} %refs_3_.1, bf16[2048]{0:T(1024)(128)(2,1)} %refs_4_.1, bf16[1,4,256,1024]{3,2,1,0:T(8,128)(2,1)} %refs_5_.1, bf16[1,4,256,1024]{3,2,1,0:T(8,128)(2,1)} %refs_6_.1, ...), custom_call_target="tpu_custom_call" | custom-call | flops 3355443200 | bytes 52428800 | tf_op jit(solution)/shard_map/layer/pallas_call | solution.py:527
  63.8 1.4 %copy.13 = bf16[4,4096]{1,0:T(4,128)(2,1)} copy(bf16[4,4096]{1,0:T(4,128)(2,1)} %layer.1) | data formatting | bytes 65536

commit v3 on v2

--- a/solution.py
+++ b/solution.py
@@ -118,7 +118,7 @@
     out_hbm, gate_hbm, up_hbm, down_hbm, out,
     w_out, w_gate, w_up, w_down, keys, values, qf, ef, att,
     xg, xf, xb, part, rs_in, stream, sq_out, sq_in, inv_all, xs,
-    gu, core_in, sum_out, x_in, hid, acc, dn, dn_in, fin, fin_in,
+    ahead, gu, core_in, sum_out, x_in, hid, acc, dn, dn_in, fin, fin_in,
     w_sem, c_sem, s1, r1, s2, r2, s3, r3, s4, r4, s5, r5, s6, r6, s7, r7,
     sa, ra, sb, rb, sc, rc_, sd, rd, s8, r8, s9, r9,
 ):
@@ -210,27 +210,34 @@
         weights[0].wait()
         for copy in weights[1:]:
             copy.start()
+        def own_copy(s):
+            mine = xg.at[:, col, s]
+            return rcopy(mine, mine, s2.at[0, s], r2.at[0, s], at(1, row, mate))
+
+        def across_copy(s, d):
+            mine = xg.at[:, col, s]
+            return rcopy(mine, mine, s2.at[d, s], r2.at[d, s], at(1, row, hi_peer(d)))
+
+        def passed_copy(s, d):
+            got = xg.at[:, hi_peer(his - d), s]
+            k = his + d - 1
+            return rcopy(got, got, s2.at[k, s], r2.at[k, s], at(1, row, mate))
+
+        for s in range(slots + 1):
+            if s < slots:
+                for d in range(rows):
+                    head_copy(s, d).wait_recv()
+                for d in range(1, his):
+                    across_copy(s, d).start()
+                own_copy(s).start()
+            if s > 0:
+                for d in range(1, his):
+                    across_copy(s - 1, d).wait_recv()
+                    passed_copy(s - 1, d).start()
         for s in range(slots):
-            for d in range(rows):
-                head_copy(s, d).wait_recv()
-        mine = xg.at[:, col]
-        own = rcopy(mine, mine, s2.at[0], r2.at[0], at(1, row, mate))
-        own.start()
-        across = [
-            rcopy(mine, mine, s2.at[d], r2.at[d], at(1, row, hi_peer(d))) for d in range(1, his)
-        ]
-        for copy in across:
-            copy.start()
-        passed = []
-        for d in range(1, his):
-            across[d - 1].wait_recv()
-            got = xg.at[:, hi_peer(his - d)]
-            copy = rcopy(got, got, s2.at[his + d - 1], r2.at[his + d - 1], at(1, row, mate))
-            copy.start()
-            passed.append(copy)
-        own.wait_recv()
-        for copy in passed:
-            copy.wait_recv()
+            own_copy(s).wait_recv()
+            for d in range(1, his):
+                passed_copy(s, d).wait_recv()
         total = rows * cols * slots
         xf[...] = xg[...].astype(F32).reshape(total * heads, HD)
         for h in range(heads):
@@ -251,6 +258,12 @@
             part[j] = res.reshape(rows, group, tile)
             for d in range(1, rows):
                 proj_copy(j, d).start()
+
+        def stream_copy(j, d):
+            chunk = xs.at[row, :, pl.ds(pl.multiple_of(j * tile, tile), tile)]
+            return rcopy(
+                chunk, chunk, s4.at[d - 1, j], r4.at[d - 1, j], at(1, row_peer(d), col)
+            )
 
         squares = jnp.zeros((group, 1), F32)
         my_rows = pl.ds(pl.multiple_of(row * group, group), group)
@@ -262,14 +275,11 @@
             lanes = slice(j * tile, (j + 1) * tile)
             value = value + residual[my_rows, lanes].astype(F32)
             stream[:, lanes] = value
+            xs[row, :, lanes] = (value * gain[lanes].astype(F32)[None, :]).astype(BF16)
+            for d in range(1, rows):
+                stream_copy(j, d).start()
             squares = squares + jnp.sum(value * value, axis=1, keepdims=True)
-            xs[row, :, lanes] = (value * gain[lanes].astype(F32)[None, :]).astype(BF16)
         sq_out[...] = jnp.broadcast_to(squares, sq_out.shape)
-
-        def stream_copy(d):
-            return rcopy(
-                xs.at[row], xs.at[row], s4.at[d - 1], r4.at[d - 1], at(1, row_peer(d), col)
-            )
 
         def square_copy(d):
             return rcopy(
@@ -284,24 +294,38 @@
 
         for d in range(1, cols):
             square_copy(d).start()
-        for d in range(1, rows):
-            stream_copy(d).start()
-        sums = sq_out[...]
-        for d in range(1, cols):
-            square_copy(d).wait_recv()
-            sums = sums + sq_in[d - 1]
-        inv_all[row] = lax.rsqrt(sums / D + eps)
-        for d in range(1, rows):
-            inv_copy(d).start()
-        for d in range(1, rows):
-            stream_copy(d).wait_recv()
+        steps, unit = gu.shape[0], gu.shape[5]
+        weights[1].wait()
+        weights[2].wait()
+
+        early = tiles // 2
+        for k in range(early):
+            for d in range(1, rows):
+                stream_copy(k, d).wait_recv()
+            lanes = slice(k * tile, (k + 1) * tile)
+            x_part = xs[:, :, lanes].reshape(rows * group, tile)
+
+            @pl.loop(0, steps)
+            def _(j):
+                at_cols = pl.ds(pl.multiple_of(j * unit, unit), unit)
+                for n, w in enumerate((w_gate, w_up)):
+                    res = jnp.dot(x_part, w[lanes, at_cols], preferred_element_type=F32)
+                    ahead[j, n] = res if k == 0 else ahead[j, n] + res
+
+            if k == 0:
+                sums = sq_out[...]
+                for d in range(1, cols):
+                    square_copy(d).wait_recv()
+                    sums = sums + sq_in[d - 1]
+                inv_all[row] = lax.rsqrt(sums / D + eps)
+                for d in range(1, rows):
+                    inv_copy(d).start()
+        for k in range(early, tiles):
+            for d in range(1, rows):
+                stream_copy(k, d).wait_recv()
         for d in range(1, rows):
             inv_copy(d).wait_recv()
-        weights[1].wait()
-        weights[2].wait()
         weights[3].wait()
-
-        steps, unit = gu.shape[0], gu.shape[5]
 
         def core_copy(j):
             return rcopy(gu.at[j, 1 - core], core_in.at[j], sa.at[j], ra.at[j], at(1, row, mate))
@@ -335,11 +359,12 @@
             @pl.when(on0)
             def _():
                 at_cols = pl.ds(pl.multiple_of(j0 * unit, unit), unit)
-                x = xs[...].reshape(rows * group, width)
+                rest = slice(early * tile, width)
+                x = xs[:, :, rest].reshape(rows * group, width - early * tile)
                 scale = inv_all[...].reshape(rows * group, HD)[:, :1]
                 for n, w in enumerate((w_gate, w_up)):
-                    res = jnp.dot(x, w[:, at_cols], preferred_element_type=F32) * scale
-                    res = res.astype(BF16)
+                    res = jnp.dot(x, w[rest, at_cols], preferred_element_type=F32)
+                    res = ((res + ahead[j0, n]) * scale).astype(BF16)
                     for q in range(cols):
                         gu[j0, q % 2, q // 2, n] = res[q * quarter : (q + 1) * quarter]
                 core_copy(j0).start()
@@ -381,38 +406,51 @@
                 hid_copy(j4, 0).wait_recv()
                 for d in range(1, his):
                     fwd_copy(j4, d).wait_recv()
+
+            @pl.when(jnp.logical_and(on4, j4 < steps - 1))
+            def _():
                 h = hid[j4].reshape(rows * group, unit)
                 w = w_down[pl.ds(pl.multiple_of(j4 * unit, unit), unit), :]
                 acc[...] += jnp.dot(h, w, preferred_element_type=F32)
 
-        dn[...] = acc[...].astype(BF16).reshape(rows, group, width)
-
-        def down_copy(d):
+        def down_copy(j, d):
             return rcopy(
-                dn.at[row_peer(d)], dn_in.at[d - 1], s7.at[d - 1], r7.at[d - 1],
+                dn.at[j, row_peer(d)], dn_in.at[d - 1, j], s7.at[d - 1, j], r7.at[d - 1, j],
                 at(1, row_peer(d), col),
             )
 
-        for d in range(1, rows):
-            down_copy(d).start()
-        last = stream[...] + dn[row].astype(F32)
-        for d in range(1, rows):
-            down_copy(d).wait_recv()
-            last = last + dn_in[d - 1].astype(F32)
-        last = last.astype(BF16).astype(F32)
-        for c in range(cols):
-            fin[c] = last[c * slots : (c + 1) * slots].astype(BF16)
-
-        own.wait_send()
-        for copy in across + passed:
-            copy.wait_send()
+        h_last = hid[steps - 1].reshape(rows * group, unit)
+
+        @pl.loop(0, tiles)
+        def _(j):
+            lanes = pl.ds(pl.multiple_of(j * tile, tile), tile)
+            w = w_down[(steps - 1) * unit : steps * unit, lanes]
+            res = acc[:, lanes] + jnp.dot(h_last, w, preferred_element_type=F32)
+            dn[j] = res.astype(BF16).reshape(rows, group, tile)
+            for d in range(1, rows):
+                down_copy(j, d).start()
+
+        for j in range(tiles):
+            lanes = slice(j * tile, (j + 1) * tile)
+            last = stream[:, lanes] + dn[j, row].astype(F32)
+            for d in range(1, rows):
+                down_copy(j, d).wait_recv()
+                last = last + dn_in[d - 1, j].astype(F32)
+            for c in range(cols):
+                fin[c, :, lanes] = last[c * slots : (c + 1) * slots].astype(BF16)
+
+        for s in range(slots):
+            own_copy(s).wait_send()
+            for d in range(1, his):
+                across_copy(s, d).wait_send()
+                passed_copy(s, d).wait_send()
         for d in range(1, rows):
             @pl.loop(0, tiles)
             def _(j):
                 proj_copy(j, d).wait_send()
-            stream_copy(d).wait_send()
+                stream_copy(j, d).wait_send()
+                down_copy(j, d).wait_send()
             inv_copy(d).wait_send()
-            down_copy(d).wait_send()
         for d in range(1, cols):
             square_copy(d).wait_send()
 
@@ -459,7 +497,7 @@
             rcopy(
                 fin.at[0], fin_in.at[k], s9.at[0], r8.at[k], at(1 - side, row, col)
             ).wait_recv()
-        out[:, k * width : (k + 1) * width] = fin_in[k]
+        out[:, k * width : (k + 1) * width] = fin_in[k].astype(F32)
 
 
 def layer(rows, cols, queries, entries, lengths, residual, gain, keys, values, out_w, gate_w, up_w, down_w):
@@ -468,7 +506,7 @@
     total, width = residual.shape
     group, quarter, his = total // rows, total // cols, cols // 2
     ff = gate_w.shape[2]
-    tile, unit = tile_of(width), tile_of(ff)
+    tile, unit = width // 4, tile_of(ff)
     tiles, steps = width // tile, ff // unit
     dma = pltpu.SemaphoreType.DMA
     vmem = pltpu.VMEM
@@ -492,24 +530,25 @@
         vmem((cols - 1, group, HD), F32),
         vmem((rows, group, HD), F32),
         vmem((rows, group, width), BF16),
+        vmem((steps, 2, total, unit), F32),
         vmem((steps, 2, his, 2, quarter, unit), BF16),
         vmem((steps, his, 2, quarter, unit), BF16),
         vmem((steps, his, 2, quarter, unit), BF16),
         vmem((his - 1, steps, 2, quarter, unit), BF16),
         vmem((steps, cols, quarter, unit), BF16),
         vmem((total, width), F32),
-        vmem((rows, group, width), BF16),
-        vmem((rows - 1, group, width), BF16),
+        vmem((tiles, rows, group, tile), BF16),
+        vmem((rows - 1, tiles, group, tile), BF16),
         vmem((cols, slots, width), BF16),
         vmem((cols // 2, slots, width), BF16),
         dma((4,)), dma((2, slots)),
         dma((slots, rows)), dma((slots, rows)),
-        dma((2 * his - 1,)), dma((2 * his - 1,)),
+        dma((2 * his - 1, slots)), dma((2 * his - 1, slots)),
         dma((rows - 1, tiles)), dma((rows - 1, tiles)),
-        dma((rows - 1,)), dma((rows - 1,)),
+        dma((rows - 1, tiles)), dma((rows - 1, tiles)),
         dma((cols - 1,)), dma((cols - 1,)),
         dma((rows - 1,)), dma((rows - 1,)),
-        dma((rows - 1,)), dma((rows - 1,)),
+        dma((rows - 1, tiles)), dma((rows - 1, tiles)),
         dma((steps,)), dma((steps,)),
         dma((his - 1, steps)), dma((his - 1, steps)),
         dma((his, steps)), dma((his, steps)),
@@ -526,7 +565,7 @@
     weight_bytes = 2 * (out_w.size + gate_w.size + up_w.size + down_w.size)
     return pl.pallas_call(
         kernel,
-        out_shape=jax.ShapeDtypeStruct((slots, width * cols // 2), BF16),
+        out_shape=jax.ShapeDtypeStruct((slots, width * cols // 2), F32),
         in_specs=[in_vmem, in_vmem, pl.BlockSpec(memory_space=pltpu.SMEM), in_vmem, in_vmem]
         + [anywhere] * 6,
         out_specs=in_vmem,
@@ -538,7 +577,7 @@
             flops=total * weight_bytes, bytes_accessed=weight_bytes, transcendentals=0
         ),
         name="layer",
-    )(queries, entries, lengths, residual, gain, keys, values, out_w, gate_w, up_w, down_w)
+    )(queries, entries, lengths, residual, gain, keys, values, out_w, gate_w, up_w, down_w).astype(BF16)
 
 
 def local(

time: 65.4 us -> 65.6 us (level)
  other arithmetic: 0 us -> 1.47 us
  local copies, waits for them, and re-layouts: 1.39 us -> 0 us
    convert_element_type x0 -> x1, other arithmetic: none -> 1.47 us  [layer(): return pl.pallas_call(kernel, out_shape=jax.ShapeDtypeStruct((slots, widt...]
    unnamed x1 -> x0, local copies, waits for them, and re-layouts: 1.39 us -> none
where the time goes in v3:
time: 65.6 us; the launch traced here: 65.4 us
  Pallas kernels  64 us (98%)
  other arithmetic  1.47 us (2%)
    pallas_call x1, Pallas kernels, layer(): pl.pallas_call(kernel, out_shape=jax.ShapeDtypeStruct((slots, width * col...  64 us
    convert_element_type x1, other arithmetic, layer(): return pl.pallas_call(kernel, out_shape=jax.ShapeDtypeStruct((slots, widt...  1.47 us

profile of v3, /device:TPU:0, one launch (start us, length us, event | category | flops | bytes accessed | tf_op | source)
XLA Modules:
  0.0 65.4 jit_solution(14570680961833994748)
XLA Ops:
  0.0 64.0 %layer.1 = f32[4,4096]{1,0:T(4,128)} custom-call(bf16[4,8192]{1,0:T(4,128)(2,1)} %refs_0_.1, bf16[4,2048]{1,0:T(4,128)(2,1)} %refs_1_.1, s32[4]{0:T(128)} %refs_2_.1, bf16[64,2048]{1,0:T(8,128)(2,1)} %refs_3_.1, bf16[2048]{0:T(1024)(128)(2,1)} %refs_4_.1, bf16[1,4,256,1024]{3,2,1,0:T(8,128)(2,1)} %refs_5_.1, bf16[1,4,256,1024]{3,2,1,0:T(8,128)(2,1)} %refs_6_.1, ...), custom_call_target="tpu_custom_call" | custom-call | flops 3355443200 | bytes 52428800 | tf_op jit(solution)/shard_map/layer/pallas_call | solution.py:566
  64.0 1.5 %convert_element_type.3 = bf16[4,4096]{1,0:T(4,128)(2,1)} convert(f32[4,4096]{1,0:T(4,128)} %layer.1) | non-fusion elementwise | flops 16384 | bytes 98304 | tf_op jit(solution)/shard_map/convert_element_type | solution.py:580

commit v4 on v3

--- a/solution.py
+++ b/solution.py
@@ -145,16 +145,25 @@
     def hi_peer(d):
         return lax.rem(hi + d, his) * 2 + core
 
-    weights = [
-        pltpu.make_async_copy(h.at[0], w, w_sem.at[i])
-        for i, (h, w) in enumerate(
-            ((out_hbm, w_out), (gate_hbm, w_gate), (up_hbm, w_up), (down_hbm, w_down))
-        )
-    ]
+    tiles, steps = part.shape[0], gu.shape[0]
+
+    def blocks_of(k, count):
+        hbm, ref = ((out_hbm, w_out), (gate_hbm, w_gate), (up_hbm, w_up), (down_hbm, w_down))[k]
+        size = ref.shape[0] // count
+
+        def block(j):
+            lines = pl.ds(pl.multiple_of(j * size, size), size)
+            return pltpu.make_async_copy(hbm.at[0, lines], ref.at[lines], w_sem.at[k, j])
+
+        return block
+
+    out_block, down_block = blocks_of(0, tiles), blocks_of(3, steps)
+    gate_block, up_block = blocks_of(1, tiles), blocks_of(2, tiles)
 
     @pl.when(side == 1)
     def _():
-        weights[0].start()
+        for k in range(tiles):
+            out_block(k).start()
 
     caches = [
         pltpu.make_async_copy(h.at[0, s], v.at[s], c_sem.at[i, s])
@@ -207,9 +216,12 @@
 
     @pl.when(side == 1)
     def _():
-        weights[0].wait()
-        for copy in weights[1:]:
-            copy.start()
+        early = tiles // 2
+        for k in range(tiles):
+            out_block(k).wait()
+        for k in range(early):
+            gate_block(k).start()
+            up_block(k).start()
         def own_copy(s):
             mine = xg.at[:, col, s]
             return rcopy(mine, mine, s2.at[0, s], r2.at[0, s], at(1, row, mate))
@@ -230,6 +242,10 @@
                 for d in range(1, his):
                     across_copy(s, d).start()
                 own_copy(s).start()
+                if s == 0:
+                    for k in range(early, tiles):
+                        gate_block(k).start()
+                        up_block(k).start()
             if s > 0:
                 for d in range(1, his):
                     across_copy(s - 1, d).wait_recv()
@@ -238,12 +254,14 @@
             own_copy(s).wait_recv()
             for d in range(1, his):
                 passed_copy(s, d).wait_recv()
+        for j in range(steps):
+            down_block(j).start()
         total = rows * cols * slots
         xf[...] = xg[...].astype(F32).reshape(total * heads, HD)
         for h in range(heads):
             xb[:, h * HD : (h + 1) * HD] = xf[pl.ds(h, total, stride=heads), :].astype(BF16)
 
-        tiles, tile = part.shape[0], part.shape[3]
+        tile = part.shape[3]
 
         def proj_copy(j, d):
             return rcopy(
@@ -251,7 +269,7 @@
                 at(1, row_peer(d), col),
             )
 
-        @pl.loop(0, tiles)
+        @pl.loop(0, tiles, unroll=True)
         def _(j):
             w = w_out[:, pl.ds(pl.multiple_of(j * tile, tile), tile)]
             res = jnp.dot(xb[...], w, preferred_element_type=F32).astype(BF16)
@@ -294,18 +312,17 @@
 
         for d in range(1, cols):
             square_copy(d).start()
-        steps, unit = gu.shape[0], gu.shape[5]
-        weights[1].wait()
-        weights[2].wait()
-
-        early = tiles // 2
+        unit = gu.shape[5]
+
         for k in range(early):
+            gate_block(k).wait()
+            up_block(k).wait()
             for d in range(1, rows):
                 stream_copy(k, d).wait_recv()
             lanes = slice(k * tile, (k + 1) * tile)
             x_part = xs[:, :, lanes].reshape(rows * group, tile)
 
-            @pl.loop(0, steps)
+            @pl.loop(0, steps, unroll=True)
             def _(j):
                 at_cols = pl.ds(pl.multiple_of(j * unit, unit), unit)
                 for n, w in enumerate((w_gate, w_up)):
@@ -321,11 +338,12 @@
                 for d in range(1, rows):
                     inv_copy(d).start()
         for k in range(early, tiles):
+            gate_block(k).wait()
+            up_block(k).wait()
             for d in range(1, rows):
                 stream_copy(k, d).wait_recv()
         for d in range(1, rows):
             inv_copy(d).wait_recv()
-        weights[3].wait()
 
         def core_copy(j):
             return rcopy(gu.at[j, 1 - core], core_in.at[j], sa.at[j], ra.at[j], at(1, row, mate))
@@ -403,6 +421,7 @@
 
             @pl.when(on4)
             def _():
+                down_block(j4).wait()
                 hid_copy(j4, 0).wait_recv()
                 for d in range(1, his):
                     fwd_copy(j4, d).wait_recv()
@@ -541,7 +560,7 @@
         vmem((rows - 1, tiles, group, tile), BF16),
         vmem((cols, slots, width), BF16),
         vmem((cols // 2, slots, width), BF16),
-        dma((4,)), dma((2, slots)),
+        dma((4, max(tiles, steps))), dma((2, slots)),
         dma((slots, rows)), dma((slots, rows)),
         dma((2 * his - 1, slots)), dma((2 * his - 1, slots)),
         dma((rows - 1, tiles)), dma((rows - 1, tiles)),

time: 65.6 us -> 65.2 us (level)
  no operation moved by 1% of the time
where the time goes in v4:
time: 65.2 us; the launch traced here: 65.1 us
  Pallas kernels  63.6 us (98%)
  other arithmetic  1.47 us (2%)
    pallas_call x1, Pallas kernels, layer(): pl.pallas_call(kernel, out_shape=jax.ShapeDtypeStruct((slots, width * col...  63.6 us
    convert_element_type x1, other arithmetic, layer(): return pl.pallas_call(kernel, out_shape=jax.ShapeDtypeStruct((slots, widt...  1.47 us

profile of v4, /device:TPU:0, one launch (start us, length us, event | category | flops | bytes accessed | tf_op | source)
XLA Modules:
  0.0 65.1 jit_solution(4500598137558630224)
XLA Ops:
  0.0 63.6 %layer.1 = f32[4,4096]{1,0:T(4,128)} custom-call(bf16[4,8192]{1,0:T(4,128)(2,1)} %refs_0_.1, bf16[4,2048]{1,0:T(4,128)(2,1)} %refs_1_.1, s32[4]{0:T(128)} %refs_2_.1, bf16[64,2048]{1,0:T(8,128)(2,1)} %refs_3_.1, bf16[2048]{0:T(1024)(128)(2,1)} %refs_4_.1, bf16[1,4,256,1024]{3,2,1,0:T(8,128)(2,1)} %refs_5_.1, bf16[1,4,256,1024]{3,2,1,0:T(8,128)(2,1)} %refs_6_.1, ...), custom_call_target="tpu_custom_call" | custom-call | flops 3355443200 | bytes 52428800 | tf_op jit(solution)/shard_map/layer/pallas_call | solution.py:585
  63.6 1.5 %convert_element_type.3 = bf16[4,4096]{1,0:T(4,128)(2,1)} convert(f32[4,4096]{1,0:T(4,128)} %layer.1) | non-fusion elementwise | flops 16384 | bytes 98304 | tf_op jit(solution)/shard_map/convert_element_type | solution.py:599
